TPU v7x, 512 devices: a whole 4x4x16 slice. The times are simulated.
512 devices in a mesh: band: 16 (over z_hi, y), grid: 32 (over z_lo, x, core).
Axes of the slice: x: 4, y: 4, z: 16 (z_hi: 4, z_lo: 4; z = z_hi * 4 + z_lo), core: 2. Of those that a mesh axis runs over, the one named last changes fastest.
Arguments:
- orbitals: bfloat16 [32, 160, 160, 160], P('band', 'grid'), may hold values from -6 to 6
- touched: int32 [2, 16], P(None, 'band'), may hold values from 0 to 1
Outputs:
- exchange_terms: float32 [32, 160, 160, 160], P('band', 'grid')
All inputs are finite; a program needn't handle non-finite values.
Results may differ from a plain program's by a relative error of at most 0.0003.
Values may be sent and summed in bfloat16 or wider, within the bound.
A program may use at most 64 MiB of HBM per device.

v0:
```python
import math

import jax
import jax.numpy as jnp
from jax import lax
from jax.sharding import PartitionSpec as P

highest = lax.Precision.HIGHEST


def shifted(block, axis, distance):
    devices = range(lax.axis_size(axis))
    route = [((i - distance) % len(devices), i) for i in devices]
    return lax.ppermute(block, axis, route)


def cas_table(length):
    wave = jnp.arange(length, dtype=jnp.int32)
    product = wave[:, None] * wave[None, :] % length
    phases = product.astype(jnp.float32) * (2.0 * math.pi / length)
    return jnp.cos(phases) + jnp.sin(phases)


def screened_slab(length, planes, first_row):
    wave = jnp.arange(length, dtype=jnp.int32)
    folded = jnp.minimum(wave, length - wave).astype(jnp.float32)
    middle = first_row + jnp.arange(planes, dtype=jnp.int32)
    folded_mid = jnp.minimum(middle, length - middle).astype(jnp.float32)
    square = (
        folded[:, None, None] ** 2 + folded_mid[None, :, None] ** 2 + folded[None, None, :] ** 2
    )
    scaled = square / (0.0003 * length * length)
    safe = jnp.where(scaled > 0, scaled, 1.0)
    factor = 100.0 * jnp.where(scaled > 0, -jnp.expm1(-safe) / safe, 1.0)
    return factor / float(length) ** 3


def convolve(densities, table, scaling):
    spread = jnp.einsum("axyz,yk->axkz", densities, table, precision=highest)
    spread = jnp.einsum("axyz,zk->axyk", spread, table, precision=highest)
    turned = (
        jnp.einsum(
            "axyz,xk->akyz",
            lax.all_to_all(spread, "grid", split_axis=2, concat_axis=1, tiled=True),
            table,
            precision=highest,
        )
        * scaling[None]
    )
    turned = jnp.einsum("akyz,kx->axyz", turned, table, precision=highest)
    mixed = lax.all_to_all(turned, "grid", split_axis=1, concat_axis=2, tiled=True)
    mixed = jnp.einsum("axkz,ky->axyz", mixed, table, precision=highest)
    return jnp.einsum("axyk,kz->axyz", mixed, table, precision=highest)


def on_device(orbitals, touched):
    own_count = orbitals.shape[0]
    planes = orbitals.shape[1]
    length = orbitals.shape[2]
    table = cas_table(length)
    scaling = screened_slab(length, planes, lax.axis_index("grid") * planes)
    lend_one = lax.dynamic_index_in_dim(orbitals, touched[0, 0], 0, keepdims=False)
    lend_two = lax.dynamic_index_in_dim(orbitals, touched[1, 0], 0, keepdims=False)
    visitor_one = shifted(lend_one, "band", 1)
    visitor_two = shifted(lend_two, "band", 2)
    widened = orbitals.astype(jnp.float32)
    guest_one = visitor_one.astype(jnp.float32)
    guest_two = visitor_two.astype(jnp.float32)
    dens_one = widened * guest_one[None]
    dens_two = widened * guest_two[None]
    pot_one = convolve(dens_one, table, scaling)
    pot_two = convolve(dens_two, table, scaling)
    result = guest_one[None] * pot_one + guest_two[None] * pot_two
    sent_one = jnp.sum(widened * pot_one, axis=0)
    sent_two = jnp.sum(widened * pot_two, axis=0)
    back_one = shifted(sent_one, "band", -1)
    back_two = shifted(sent_two, "band", -2)
    positions = jnp.arange(own_count, dtype=jnp.int32)
    mask_one = (positions == touched[0, 0]).astype(jnp.float32)[:, None, None, None]
    mask_two = (positions == touched[1, 0]).astype(jnp.float32)[:, None, None, None]
    return result + mask_one * back_one[None] + mask_two * back_two[None]


def solution(mesh):
    in_specs = (P("band", "grid", None, None), P(None, "band"))
    out_specs = P("band", "grid", None, None)
    return jax.shard_map(
        on_device, mesh=mesh, in_specs=in_specs, out_specs=out_specs, check_vma=False
    )
```

profile of v0, /device:TPU:21, one launch (start us, length us, event | category | flops | bytes accessed | tf_op | source)
XLA Modules:
  0.0 440.9 jit_solution(7541665031042367441)
XLA Ops:
  6.9 8.5 %collective-permute-start.1 = (bf16[5,160,160]{2,1,0:T(8,128)(2,1)S(1)}, bf16[5,160,160]{2,1,0:T(8,128)(2,1)S(1)}, u32[]{:S(2)}, u32[]{:S(2)}) collective-permute-start(bf16[5,160,160]{2,1,0:T(8,128)(2,1)S(1)} %get-tuple-element.8), channel_id=1, source_target_pairs={{448,0},{480,32},{0,64},{32,96},{64,128},{96,160},{128,192},{160,2... | collective-permute-start | bytes 768008 | tf_op jit(solution)/shard_map/ppermute | solution.py:14
  15.4 12.8 %collective-permute-done.1 = bf16[5,160,160]{2,1,0:T(8,128)(2,1)S(1)} collective-permute-done((bf16[5,160,160]{2,1,0:T(8,128)(2,1)S(1)}, bf16[5,160,160]{2,1,0:T(8,128)(2,1)S(1)}, u32[]{:S(2)}, u32[]{:S(2)}) %collective-permute-start.1) | collective-permute-done | bytes 256032 | tf_op jit(solution)/shard_map/ppermute | solution.py:14
  32.7 2.4 copy.51
  35.1 30.5 %all-to-all-start.2 = ((f32[2,5,160,160]{3,0,1,2:T(2,128)}), f32[2,5,160,160]{3,0,1,2:T(2,128)S(1)}, u32[]{:S(2)}, u32[]{:S(2)}) async-start(f32[2,5,160,160]{3,0,1,2:T(2,128)} %copy.51), calls=%async_computation.2 | async-start | bytes 3276800 | tf_op jit(solution)/shard_map/all_to_all | solution.py:44
  65.7 4.1 collective-permute-start
  69.8 12.7 %collective-permute-done = bf16[5,160,160]{2,1,0:T(8,128)(2,1)S(1)} collective-permute-done((bf16[5,160,160]{2,1,0:T(8,128)(2,1)}, bf16[5,160,160]{2,1,0:T(8,128)(2,1)S(1)}, u32[]{:S(2)}, u32[]{:S(2)}) %collective-permute-start) | collective-permute-done | bytes 256032 | tf_op jit(solution)/shard_map/ppermute | solution.py:14
  87.8 2.5 copy.40
  90.3 13.4 %all-to-all-done.2 = f32[2,5,160,160]{3,0,1,2:T(2,128)S(1)} async-done(((f32[2,5,160,160]{3,0,1,2:T(2,128)}), f32[2,5,160,160]{3,0,1,2:T(2,128)S(1)}, u32[]{:S(2)}, u32[]{:S(2)}) %all-to-all-start.2) | async-done | bytes 1024032 | tf_op jit(solution)/shard_map/all_to_all | solution.py:44
  104.9 7.2 %all-to-all-start = ((f32[2,5,160,160]{3,0,1,2:T(2,128)}), f32[2,5,160,160]{3,0,1,2:T(2,128)}, u32[]{:S(2)}, u32[]{:S(2)}) async-start(f32[2,5,160,160]{3,0,1,2:T(2,128)} %copy.40), calls=%async_computation | async-start | bytes 3276800 | tf_op jit(solution)/shard_map/all_to_all | solution.py:44
  114.8 2.2 fusion.18
  119.2 2.4 copy.57
  121.6 28.4 %all-to-all-done = f32[2,5,160,160]{3,0,1,2:T(2,128)} async-done(((f32[2,5,160,160]{3,0,1,2:T(2,128)}), f32[2,5,160,160]{3,0,1,2:T(2,128)}, u32[]{:S(2)}, u32[]{:S(2)}) %all-to-all-start) | async-done | bytes 1024032 | tf_op jit(solution)/shard_map/all_to_all | solution.py:44
  150.1 6.9 %all-to-all-start.3 = ((f32[2,160,5,160]{3,0,2,1:T(2,128)}), f32[2,160,5,160]{3,0,2,1:T(2,128)}, u32[]{:S(2)}, u32[]{:S(2)}) async-start(f32[2,160,5,160]{3,0,2,1:T(2,128)} %copy.57), calls=%async_computation.3 | async-start | bytes 3276800 | tf_op jit(solution)/shard_map/all_to_all | solution.py:51
  158.9 2.2 fusion.22
  163.4 2.5 copy.46
  165.8 29.0 %all-to-all-done.3 = f32[2,160,5,160]{3,0,2,1:T(2,128)} async-done(((f32[2,160,5,160]{3,0,2,1:T(2,128)}), f32[2,160,5,160]{3,0,2,1:T(2,128)}, u32[]{:S(2)}, u32[]{:S(2)}) %all-to-all-start.3) | async-done | bytes 1024032 | tf_op jit(solution)/shard_map/all_to_all | solution.py:51
  194.9 6.9 %all-to-all-start.1 = ((f32[2,160,5,160]{3,0,2,1:T(2,128)}), f32[2,160,5,160]{3,0,2,1:T(2,128)}, u32[]{:S(2)}, u32[]{:S(2)}) async-start(f32[2,160,5,160]{3,0,2,1:T(2,128)} %copy.46), calls=%async_computation.1 | async-start | bytes 3276800 | tf_op jit(solution)/shard_map/all_to_all | solution.py:51
  208.1 31.6 %all-to-all-done.1 = f32[2,160,5,160]{3,0,2,1:T(2,128)} async-done(((f32[2,160,5,160]{3,0,2,1:T(2,128)}), f32[2,160,5,160]{3,0,2,1:T(2,128)}, u32[]{:S(2)}, u32[]{:S(2)}) %all-to-all-start.1) | async-done | bytes 1024032 | tf_op jit(solution)/shard_map/all_to_all | solution.py:51
  241.7 2.2 fusion.20
  244.0 2.4 fusion.2
  246.3 7.1 %collective-permute-start.2 = (f32[5,160,160]{2,1,0:T(8,128)S(1)}, f32[5,160,160]{2,1,0:T(8,128)S(1)}, u32[]{:S(2)}, u32[]{:S(2)}) collective-permute-start(f32[5,160,160]{2,1,0:T(8,128)S(1)} %get-tuple-element.5), channel_id=1, source_target_pairs={{32,0},{64,32},{96,64},{128,96},{160,128},{192,160},{224,192},{256... | collective-permute-start | bytes 1536008 | tf_op jit(solution)/shard_map/ppermute | solution.py:14
  253.4 42.6 %collective-permute-start.3 = (f32[5,160,160]{2,1,0:T(8,128)S(1)}, f32[5,160,160]{2,1,0:T(8,128)S(1)}, u32[]{:S(2)}, u32[]{:S(2)}) collective-permute-start(f32[5,160,160]{2,1,0:T(8,128)S(1)} %get-tuple-element.6), channel_id=1, source_target_pairs={{64,0},{96,32},{128,64},{160,96},{192,128},{224,160},{256,192},{28... | collective-permute-start | bytes 1536008 | tf_op jit(solution)/shard_map/ppermute | solution.py:14
  297.3 10.8 %collective-permute-done.2 = f32[5,160,160]{2,1,0:T(8,128)S(1)} collective-permute-done((f32[5,160,160]{2,1,0:T(8,128)S(1)}, f32[5,160,160]{2,1,0:T(8,128)S(1)}, u32[]{:S(2)}, u32[]{:S(2)}) %collective-permute-start.2) | collective-permute-done | bytes 512032 | tf_op jit(solution)/shard_map/ppermute | solution.py:14
  308.1 130.9 %collective-permute-done.3 = f32[5,160,160]{2,1,0:T(8,128)S(1)} collective-permute-done((f32[5,160,160]{2,1,0:T(8,128)S(1)}, f32[5,160,160]{2,1,0:T(8,128)S(1)}, u32[]{:S(2)}, u32[]{:S(2)}) %collective-permute-start.3) | collective-permute-done | bytes 512032 | tf_op jit(solution)/shard_map/ppermute | solution.py:14
  (30 shorter events, 34.4 us)
Async XLA Ops:
  0.0 28.3 %copy-start = (bf16[2,5,160,160]{3,2,1,0:T(8,128)(2,1)S(1)}, bf16[2,5,160,160]{3,2,1,0:T(8,128)(2,1)}, u32[]{:S(2)}) copy-start(bf16[2,5,160,160]{3,2,1,0:T(8,128)(2,1)} %param.2) | copy-start | bytes 1536004
  6.9 21.4 %collective-permute-start.1 = (bf16[5,160,160]{2,1,0:T(8,128)(2,1)S(1)}, bf16[5,160,160]{2,1,0:T(8,128)(2,1)S(1)}, u32[]{:S(2)}, u32[]{:S(2)}) collective-permute-start(bf16[5,160,160]{2,1,0:T(8,128)(2,1)S(1)} %get-tuple-element.8), channel_id=1, source_target_pairs={{448,0},{480,32},{0,64},{32,96},{64,128},{96,160},{128,192},{160,2... | collective-permute-start | bytes 768008 | tf_op jit(solution)/shard_map/ppermute | solution.py:14
  35.1 68.6 %all-to-all-start.2 = ((f32[2,5,160,160]{3,0,1,2:T(2,128)}), f32[2,5,160,160]{3,0,1,2:T(2,128)S(1)}, u32[]{:S(2)}, u32[]{:S(2)}) async-start(f32[2,5,160,160]{3,0,1,2:T(2,128)} %copy.51), calls=%async_computation.2 | async-start | bytes 3276800 | tf_op jit(solution)/shard_map/all_to_all | solution.py:44
  65.7 16.8 %collective-permute-start = (bf16[5,160,160]{2,1,0:T(8,128)(2,1)}, bf16[5,160,160]{2,1,0:T(8,128)(2,1)S(1)}, u32[]{:S(2)}, u32[]{:S(2)}) collective-permute-start(bf16[5,160,160]{2,1,0:T(8,128)(2,1)} %get-tuple-element.7), channel_id=1, source_target_pairs={{480,0},{0,32},{32,64},{64,96},{96,128},{128,160},{160,192},{192,2... | collective-permute-start | bytes 768008 | tf_op jit(solution)/shard_map/ppermute | solution.py:14
  82.6 0.9 copy-start.1
  103.7 1.2 copy-start.3
  104.9 45.2 %all-to-all-start = ((f32[2,5,160,160]{3,0,1,2:T(2,128)}), f32[2,5,160,160]{3,0,1,2:T(2,128)}, u32[]{:S(2)}, u32[]{:S(2)}) async-start(f32[2,5,160,160]{3,0,1,2:T(2,128)} %copy.40), calls=%async_computation | async-start | bytes 3276800 | tf_op jit(solution)/shard_map/all_to_all | solution.py:44
  150.1 44.8 %all-to-all-start.3 = ((f32[2,160,5,160]{3,0,2,1:T(2,128)}), f32[2,160,5,160]{3,0,2,1:T(2,128)}, u32[]{:S(2)}, u32[]{:S(2)}) async-start(f32[2,160,5,160]{3,0,2,1:T(2,128)} %copy.57), calls=%async_computation.3 | async-start | bytes 3276800 | tf_op jit(solution)/shard_map/all_to_all | solution.py:51
  194.9 44.9 %all-to-all-start.1 = ((f32[2,160,5,160]{3,0,2,1:T(2,128)}), f32[2,160,5,160]{3,0,2,1:T(2,128)}, u32[]{:S(2)}, u32[]{:S(2)}) async-start(f32[2,160,5,160]{3,0,2,1:T(2,128)} %copy.46), calls=%async_computation.1 | async-start | bytes 3276800 | tf_op jit(solution)/shard_map/all_to_all | solution.py:51
  244.0 195.0 %copy-start.2 = (f32[5,160,160]{2,1,0:T(8,128)S(1)}, f32[5,160,160]{2,1,0:T(8,128)}, u32[]{:S(2)}) copy-start(f32[5,160,160]{2,1,0:T(8,128)} %copy-done.1) | copy-start | bytes 1536004
  246.3 61.7 %collective-permute-start.2 = (f32[5,160,160]{2,1,0:T(8,128)S(1)}, f32[5,160,160]{2,1,0:T(8,128)S(1)}, u32[]{:S(2)}, u32[]{:S(2)}) collective-permute-start(f32[5,160,160]{2,1,0:T(8,128)S(1)} %get-tuple-element.5), channel_id=1, source_target_pairs={{32,0},{64,32},{96,64},{128,96},{160,128},{192,160},{224,192},{256... | collective-permute-start | bytes 1536008 | tf_op jit(solution)/shard_map/ppermute | solution.py:14
  253.4 185.6 %collective-permute-start.3 = (f32[5,160,160]{2,1,0:T(8,128)S(1)}, f32[5,160,160]{2,1,0:T(8,128)S(1)}, u32[]{:S(2)}, u32[]{:S(2)}) collective-permute-start(f32[5,160,160]{2,1,0:T(8,128)S(1)} %get-tuple-element.6), channel_id=1, source_target_pairs={{64,0},{96,32},{128,64},{160,96},{192,128},{224,160},{256,192},{28... | collective-permute-start | bytes 1536008 | tf_op jit(solution)/shard_map/ppermute | solution.py:14
where the time goes:
time: 447 us; the launch traced here: 441 us
  waiting for transfers between devices  270 us (60%)
  starting transfers between devices  114 us (26%)
  matrix products  26.4 us (6%)
  local copies, waits for them, and re-layouts  23.2 us (5%)
    ppermute x4, waiting for transfers between devices, shifted(): return lax.ppermute(block, axis, route)  167 us
    ppermute x4, starting transfers between devices, shifted(): return lax.ppermute(block, axis, route)  62.3 us
    all_to_all x2, waiting for transfers between devices, convolve(): lax.all_to_all(turned, 'grid', split_axis=1, concat_axis=2, tiled=True)  60.6 us
    all_to_all x2, waiting for transfers between devices, convolve(): lax.all_to_all(spread, 'grid', split_axis=2, concat_axis=1, tiled=True)  41.8 us
    all_to_all x2, starting transfers between devices, convolve(): lax.all_to_all(spread, 'grid', split_axis=2, concat_axis=1, tiled=True)  37.7 us
    all_to_all x2, starting transfers between devices, convolve(): lax.all_to_all(turned, 'grid', split_axis=1, concat_axis=2, tiled=True)  13.8 us
  transfers between devices with their start and end apart: 8, of which 8 were waited for; matrix products, arithmetic and copies ran while one was open for 7% of the time, Pallas kernels for 0%

commit v1 on v0

v1 whole, which is shorter than its diff:
```python
import functools

import jax
import jax.numpy as jnp
import ml_dtypes
import numpy as np
from jax import lax
from jax.experimental import pallas as pl
from jax.experimental.pallas import tpu as pltpu
from jax.sharding import PartitionSpec as P

MESH = pl.DeviceIdType.MESH
F32, BF16, I16, I32 = jnp.float32, jnp.bfloat16, jnp.int16, jnp.int32

N = 160
G = 32
PL = 5
ROWS = 32
PACKED = 1008
CHUNK = ((0, 256), (256, 256), (512, 256), (768, 240))
FLOWS = ((0, 3, 0), (1, 2, 0), (1, 3, 1))
FULL = 32000.0


def split(x):
    hi = x.astype(BF16)
    return hi, (x - hi.astype(F32)).astype(BF16)


def dot(a, b):
    return jnp.dot(a, b, preferred_element_type=F32)


def dot_left(table, x):
    hi, lo = split(x)
    return dot(table[0], hi) + dot(table[0], lo) + dot(table[1], hi)


def dot_right(hi, lo, table):
    return dot(hi, table[0]) + dot(lo, table[0]) + dot(hi, table[1])


def exponent_of(largest):
    return jnp.ceil(8.0 * jnp.log2(jnp.maximum(largest, 1e-30)))


def step_up(e):
    return FULL * jnp.exp2(-0.125 * e)


def step_down(e):
    return jnp.exp2(0.125 * e) * (1.0 / FULL)


def iota(shape, axis):
    return lax.broadcasted_iota(I32, shape, axis)


def every(start, size):
    return pl.ds(start, size, stride=ROWS)


def to_i16(x):
    return x.astype(I32).astype(I16)


def kernel(
    orb, touched, ty, tyi, tx, txi, tz, tzi, out,
    lend, seen, vis, relay_f, ret, ret_send, ret_got, relay_b,
    c, send32, recv32, dhi, dlo, quant, grid_v,
    send_f, recv_f, send_b, recv_b,
    v_send, v_recv, vr_send, vr_recv, r_send, r_recv, rr_send, rr_recv,
    f_send, f_recv, b_send, b_recv,
):
    b, g = lax.axis_index("band"), lax.axis_index("grid")
    zh, y = b // 4, b % 4
    up, down = (zh + 1) % 4, (zh + 3) % 4
    lane32 = iota((G, 128), 1)
    group32 = lane32 // 32

    barrier = pltpu.get_barrier_semaphore()

    def greet_grid(i, _):
        pl.semaphore_signal(barrier, inc=1, device_id=(b, (g + i) % G), device_id_type=MESH)
        return 0

    for d in range(1, 4):
        pl.semaphore_signal(barrier, inc=1, device_id=(zh * 4 + (y + d) % 4, g), device_id_type=MESH)
    for block in (up, down):
        for yy in range(4):
            pl.semaphore_signal(barrier, inc=1, device_id=(block * 4 + yy, g), device_id_type=MESH)
    lax.fori_loop(1, G, greet_grid, 0)

    def pack(plane, store):
        tails = []
        for x in range(PL):
            v = plane(x)
            store(x * N, N, v[:, :128])
            tails.append(v[:, 128:N])
        store(PL * N, N, jnp.concatenate(tails[:4], axis=1))
        t = tails[4]
        rest = jnp.concatenate([t[144:160], jnp.zeros((32, 32), F32)], axis=0)
        return jnp.concatenate([t[0:48], t[48:96], t[96:144], rest], axis=1)

    def unpack(x, load):
        main = load(x * N, N)
        if x < 4:
            tail = load(PL * N, N)[:, 32 * x : 32 * x + 32]
        else:
            last = load(6 * N, 48)
            tail = jnp.concatenate(
                [last[:, 0:32], last[:, 32:64], last[:, 64:96], last[0:16, 96:128]], axis=0
            )
        return jnp.concatenate([main, tail], axis=1)

    for r in range(2):
        chosen = touched[r, 0]

        def lent(x, chosen=chosen):
            pick = jnp.full((N, N), chosen, I32) == 0
            return jnp.where(pick, orb[0, x].astype(F32), orb[1, x].astype(F32))

        def put(start, size, v, r=r):
            lend[r, start : start + size, :] = v.astype(BF16)

        put(6 * N, 48, pack(lent, put))

    pl.semaphore_wait(barrier, 42)

    def copy(src, dst, s, q, device):
        return pltpu.make_async_remote_copy(
            src_ref=src, dst_ref=dst, send_sem=s, recv_sem=q, device_id=device, device_id_type=MESH
        )

    def landed(ref, sem):
        pltpu.make_async_copy(ref, ref, sem).wait()

    def ship(r, forward, src, dst, s, q, relay, rs, rq):
        ahead = r + 1 if forward else -r - 1
        inside = y + ahead < 4 if forward else y + ahead >= 0
        block = up if forward else down

        @pl.when(inside)
        def _():
            copy(src.at[r], dst.at[r], s.at[r], q.at[r], (b + ahead, g)).start()

        for f, (fr, low, high) in enumerate(FLOWS):
            if fr != r:
                continue
            begin, end = (low, high) if forward else (high, low)

            @pl.when(y == begin)
            def _():
                for col, (start, size) in enumerate(CHUNK):
                    part = src.at[r, pl.ds(start, size)]
                    if col == begin:
                        goal = dst.at[r, pl.ds(start, size)]
                        copy(part, goal, s.at[r], q.at[r], (block * 4 + end, g)).start()
                    else:
                        goal = relay.at[f, pl.ds(0, size)]
                        copy(part, goal, s.at[r], rq.at[f], (zh * 4 + col, g)).start()

    def pass_on(r, forward, dst, q, relay, rs, rq):
        block = up if forward else down
        for f, (fr, low, high) in enumerate(FLOWS):
            if fr != r:
                continue
            begin, end = (low, high) if forward else (high, low)
            for col, (start, size) in enumerate(CHUNK):
                if col == begin:
                    continue

                @pl.when(y == col)
                def _():
                    part = relay.at[f, pl.ds(0, size)]
                    landed(part, rq.at[f])
                    goal = dst.at[r, pl.ds(start, size)]
                    copy(part, goal, rs.at[f], q.at[r], (block * 4 + end, g)).start()

    def shipped(forward, src, s, relay, rs):
        for r in range(2):
            landed(src.at[r], s.at[r])
        for f, (fr, low, high) in enumerate(FLOWS):
            begin = low if forward else high
            for col, (start, size) in enumerate(CHUNK):
                if col == begin:
                    continue

                @pl.when(y == col)
                def _():
                    landed(relay.at[f, pl.ds(0, size)], rs.at[f])

    for r in range(2):
        ship(r, True, lend, seen, v_send, v_recv, relay_f, vr_send, vr_recv)
    for r in range(2):
        pass_on(r, True, seen, v_recv, relay_f, vr_send, vr_recv)

    def fill(j, _):
        def squared(k):
            q = jnp.minimum(k, N - k).astype(F32)
            return q * q

        kz = jnp.minimum(iota((N, 256), 1), N)
        square = squared(iota((N, 256), 0)) + squared(kz)
        ky = 32 * j + g
        q2 = jnp.minimum(ky, N - ky).astype(F32)
        s = (square + q2 * q2) * (1.0 / (0.0003 * N * N))
        safe = jnp.where(s > 0, s, 1.0)
        factor = jnp.where(s > 0, (1.0 - jnp.exp(-safe)) / safe, 1.0)
        c[j] = factor * (100.0 / float(N) ** 3)
        return 0

    lax.fori_loop(0, PL, fill, 0)

    def see(r):
        landed(seen.at[r], v_recv.at[r])
        for x in range(PL):
            vis[r, x] = unpack(x, lambda start, size: seen[r, start : start + size, :].astype(F32))

    def send_all(a, src, dst, s, q):
        own = pl.ds(pl.multiple_of(g * ROWS, ROWS), ROWS)
        dst[a, own, :] = src[a, own, :]

        def start(i, _):
            p = (g + i) % G
            copy(
                src.at[a, pl.ds(pl.multiple_of(p * ROWS, ROWS), ROWS)],
                dst.at[a, own],
                s.at[a],
                q.at[a],
                (b, p),
            ).start()
            return 0

        lax.fori_loop(1, G, start, 0)

    def all_landed(a, ref, sem):
        part = ref.at[a, pl.ds(0, (G - 1) * ROWS)]
        pltpu.make_async_copy(part, part, sem.at[a]).wait()

    def stage_a(r, band):
        a = 2 * r + band

        def plane(x, carry):
            tail4, last = carry
            density = orb[band, x].astype(F32) * vis[r, x]
            spread = dot_left((ty[0], ty[1]), density)
            largest = jnp.max(jnp.abs(spread), axis=1, keepdims=True)
            e = exponent_of(largest)
            q = jnp.round(spread * step_up(e))
            tails = []
            for j in range(PL):
                part = q[32 * j : 32 * j + 32]
                send32[every(5 * x + j, G), :] = part[:, :128]
                tails.append(part[:, 128:N])
                last = jnp.where(lane32 == 32 + 5 * x + j, e[32 * j : 32 * j + 32], last)
            send32[every(25 + x, G), :] = jnp.concatenate(tails[:4], axis=1)
            spare = jnp.concatenate([tails[4]] * 4, axis=1)
            tail4 = jnp.where(group32 == x, spare, tail4)
            last = jnp.where(group32 + 4 == x, spare, last)
            return tail4, last

        zero = jnp.zeros((G, 128), F32)
        tail4, last = lax.fori_loop(0, PL, plane, (zero, zero))
        send32[every(30, G), :] = tail4
        send32[every(31, G), :] = last
        send_f[a] = to_i16(send32[...])
        send_all(a, send_f, recv_f, f_send, f_recv)

    def scales():
        return step_down(recv32[every(31, G), :])

    def scale_of(down_by, x, j):
        at = 32 + 5 * x + j
        return down_by[:, at : at + 1]

    def last_tail(x):
        if x == 4:
            return recv32[every(31, G), :]
        t = recv32[every(30, G), :]
        return pltpu.roll(t, 128 - 32 * x, 1) if x else t

    def stage_b(a):
        all_landed(a, recv_f, f_recv)
        recv32[...] = recv_f[a].astype(F32)
        down_by = scales()
        for x in range(PL):
            rows = slice(32 * x, 32 * x + 32)
            by = [scale_of(down_by, x, j) for j in range(PL)]
            mixed = jnp.where(
                group32 == 0, by[0], jnp.where(group32 == 1, by[1], jnp.where(group32 == 2, by[2], by[3]))
            )
            t_hi, t_lo = split(recv32[every(25 + x, G), :] * mixed)
            for j in range(PL):
                hi, lo = split(recv32[every(5 * x + j, G), :] * by[j])
                dhi[j, rows, :128] = hi
                dlo[j, rows, :128] = lo
                if j == 4:
                    t_hi, t_lo = split(last_tail(x) * by[4])
                dhi[j, rows, 128:] = t_hi
                dlo[j, rows, 128:] = t_lo

        def row(j, last):
            v = j % 4
            z = dot_right(dhi[j], dlo[j], (tz[0, v], tz[1, v]))
            w = dot_left((tx[0], tx[1]), z) * c[j]
            u = dot_left((txi[0], txi[1]), w)
            hi, lo = split(u)
            o = dot_right(hi, lo, (tzi[0, v], tzi[1, v]))
            e = exponent_of(jnp.max(jnp.abs(o), axis=1, keepdims=True))
            quant[j] = jnp.round(o * step_up(e))
            for x in range(PL):
                last = jnp.where(lane32 == 32 + 5 * x + j, e[32 * x : 32 * x + 32], last)
            return last

        last = lax.fori_loop(0, PL, row, jnp.zeros((G, 128), F32))
        tail4 = jnp.zeros((G, 128), F32)
        for x in range(PL):
            rows = slice(32 * x, 32 * x + 32)
            for j in range(PL):
                send32[every(5 * x + j, G), :] = quant[j, rows, :128]
            send32[every(25 + x, G), :] = (
                quant[0, rows, 128:] + quant[1, rows, 128:] + quant[2, rows, 128:] + quant[3, rows, 128:]
            )
            t = quant[4, rows, 128:]
            if x == 4:
                last = last + t
            else:
                tail4 = tail4 + (pltpu.roll(t, 32 * x, 1) if x else t)
        send32[every(30, G), :] = tail4
        send32[every(31, G), :] = last
        send_b[a] = to_i16(send32[...])
        send_all(a, send_b, recv_b, b_send, b_recv)

    def stage_c(r, band):
        a = 2 * r + band
        all_landed(a, recv_b, b_recv)
        recv32[...] = recv_b[a].astype(F32)
        down_by = scales()
        for x in range(PL):
            t = recv32[every(25 + x, G), :]
            for j in range(PL):
                rows = slice(32 * j, 32 * j + 32)
                by = scale_of(down_by, x, j)
                grid_v[x, rows, :128] = recv32[every(5 * x + j, G), :] * by
                if j == 4:
                    tail = last_tail(x)
                else:
                    tail = pltpu.roll(t, 128 - 32 * j, 1) if j else t
                grid_v[x, rows, 128:] = tail * by

        def plane(x, _):
            potential = dot_left((tyi[0], tyi[1]), grid_v[x])[:, :N]
            added = vis[r, x] * potential
            back = orb[band, x].astype(F32) * potential
            out[band, x] = added if r == 0 else out[band, x] + added
            ret[x] = back if band == 0 else ret[x] + back
            return 0

        lax.fori_loop(0, PL, plane, 0)

    def give_back(r):
        exps = []

        def scaled(x):
            v = ret[x]
            largest = jnp.max(jnp.max(jnp.abs(v), axis=1, keepdims=True), axis=0, keepdims=True)
            e = exponent_of(largest)
            exps.append(e)
            return jnp.round(v * step_up(e))

        def put(start, size, v):
            ret_send[r, start : start + size, :] = to_i16(v)

        last = pack(scaled, put)
        free = iota((48, 128), 0) >= 16
        lane = iota((48, 128), 1)
        for x in range(PL):
            last = jnp.where(free & (lane == 96 + x), exps[x], last)
        put(6 * N, 48, last)
        ship(r, False, ret_send, ret_got, r_send, r_recv, relay_b, rr_send, rr_recv)

    def take_back(r):
        landed(ret_got.at[r], r_recv.at[r])
        chosen = touched[r, 0]
        tail = step_down(ret_got[r, 6 * N : 6 * N + 48, :].astype(F32)[16:24])
        for x in range(PL):
            by = tail[0:1, 96 + x : 97 + x]
            v = unpack(x, lambda start, size: ret_got[r, start : start + size, :].astype(F32)) * by
            mine = jnp.full((N, N), chosen, I32) == 0
            out[0, x] = out[0, x] + jnp.where(mine, v, 0.0)
            out[1, x] = out[1, x] + jnp.where(mine, 0.0, v)

    see(0)
    stage_a(0, 0)
    stage_a(0, 1)
    see(1)
    stage_a(1, 0)
    stage_a(1, 1)
    for a in range(4):
        stage_b(a)
    stage_c(0, 0)
    stage_c(0, 1)
    give_back(0)
    stage_c(1, 0)
    stage_c(1, 1)
    give_back(1)
    for r in range(2):
        pass_on(r, False, ret_got, r_recv, relay_b, rr_send, rr_recv)
    for r in range(2):
        take_back(r)
    for a in range(4):
        all_landed(a, send_f, f_send)
        all_landed(a, send_b, b_send)
    shipped(True, lend, v_send, relay_f, vr_send)
    shipped(False, ret_send, r_send, relay_b, rr_send)


def pair(table):
    hi = table.astype(ml_dtypes.bfloat16)
    lo = (table - hi.astype(np.float64)).astype(ml_dtypes.bfloat16)
    return np.stack([hi, lo])


def tables():
    k = np.arange(N)
    phase = (k[:, None] * k[None, :] % N) * (2.0 * np.pi / N)
    cas = np.cos(phase) + np.sin(phase)
    by_plane = (5 * np.arange(G)[None, :] + np.arange(PL)[:, None]).reshape(-1)
    ty = cas
    tx = cas[:, by_plane]
    tz = np.zeros((4, 256, 256))
    tzi = np.zeros((4, 256, 256))
    for v in range(4):
        at = 128 + 32 * v
        tz[v, :128, :N] = cas[:128]
        tz[v, at : at + 32, :N] = cas[128:]
        tzi[v, :N, :128] = cas[:, :128]
        tzi[v, :N, at : at + 32] = cas[:, 128:]
    return [pair(t) for t in (ty, ty.T, tx, tx.T, tz, tzi)]


def on_device(orbitals, touched):
    vmem, smem = pl.BlockSpec(memory_space=pltpu.VMEM), pl.BlockSpec(memory_space=pltpu.SMEM)
    dma = pltpu.SemaphoreType.DMA
    message = (4, G * ROWS, 128)
    return pl.pallas_call(
        kernel,
        out_shape=jax.ShapeDtypeStruct((2, PL, N, N), F32),
        in_specs=[vmem, smem] + [vmem] * 6,
        out_specs=vmem,
        scratch_shapes=[
            pltpu.VMEM((2, PACKED, 128), BF16),
            pltpu.VMEM((2, PACKED, 128), BF16),
            pltpu.VMEM((2, PL, N, N), F32),
            pltpu.VMEM((3, 256, 128), BF16),
            pltpu.VMEM((PL, N, N), F32),
            pltpu.VMEM((2, PACKED, 128), I16),
            pltpu.VMEM((2, PACKED, 128), I16),
            pltpu.VMEM((3, 256, 128), I16),
            pltpu.VMEM((PL, N, 256), F32),
            pltpu.VMEM((G * ROWS, 128), F32),
            pltpu.VMEM((G * ROWS, 128), F32),
            pltpu.VMEM((PL, N, 256), BF16),
            pltpu.VMEM((PL, N, 256), BF16),
            pltpu.VMEM((PL, N, 256), F32),
            pltpu.VMEM((PL, N, 256), F32),
            pltpu.VMEM(message, I16),
            pltpu.VMEM(message, I16),
            pltpu.VMEM(message, I16),
            pltpu.VMEM(message, I16),
            dma((2,)), dma((2,)), dma((3,)), dma((3,)),
            dma((2,)), dma((2,)), dma((3,)), dma((3,)),
            dma((4,)), dma((4,)), dma((4,)), dma((4,)),
        ],
        compiler_params=pltpu.CompilerParams(
            collective_id=0, has_side_effects=True, vmem_limit_bytes=44 << 20
        ),
        name="exchange",
    )(orbitals, touched, *[jnp.asarray(t) for t in tables()])


def solution(mesh):
    in_specs = (P("band", "grid", None, None), P(None, "band"))
    out_specs = P("band", "grid", None, None)
    return jax.shard_map(
        on_device, mesh=mesh, in_specs=in_specs, out_specs=out_specs, check_vma=False
    )
```

time: 447 us -> 115 us (0.26)
  the two profiles are of different devices: /device:TPU:21 before, /device:TPU:56 now
where the time goes in v1:
time: 115 us
  Pallas kernels  106 us (92%)
  local copies, waits for them, and re-layouts  8.25 us (7%)
    pallas_call x1, Pallas kernels, on_device(): pl.pallas_call(kernel, out_shape=jax.ShapeDtypeStruct((2, PL, N, N), F32)...  106 us
    unnamed x14, local copies, waits for them, and re-layouts  8.25 us

profile of v1, /device:TPU:56, one launch (start us, length us, event | category | flops | bytes accessed | tf_op | source)
XLA Modules:
  0.0 114.6 jit_solution(8539140994344622506)
XLA Ops:
  0.0 0.7 copy.9.touched
  0.7 0.0 copy-start
  0.7 1.2 %copy-done = bf16[2,4,256,256]{3,2,1,0:T(8,128)(2,1)S(1)} copy-done((bf16[2,4,256,256]{3,2,1,0:T(8,128)(2,1)S(1)}, bf16[2,4,256,256]{3,2,1,0:T(8,128)(2,1)}, u32[]{:S(2)}) %copy-start) | copy-done | bytes 1048600
  2.0 0.0 copy-start.1
  2.0 1.2 %copy-done.1 = bf16[2,4,256,256]{3,2,1,0:T(8,128)(2,1)S(1)} copy-done((bf16[2,4,256,256]{3,2,1,0:T(8,128)(2,1)S(1)}, bf16[2,4,256,256]{3,2,1,0:T(8,128)(2,1)}, u32[]{:S(2)}) %copy-start.1) | copy-done | bytes 1048600
  3.2 0.0 copy-start.2
  3.2 1.1 copy-done.2
  4.3 0.0 copy-start.3
  4.3 0.9 copy-done.3
  5.3 0.0 copy-start.4
  5.3 0.9 copy-done.4
  6.2 0.0 copy-start.5
  6.2 0.9 copy-done.5
  7.1 106.3 %exchange.1 = f32[2,5,160,160]{3,2,1,0:T(8,128)S(1)} custom-call(bf16[2,5,160,160]{3,2,1,0:T(8,128)(2,1)S(1)} %copy-done.2, s32[2,1]{1,0:T(2,128)S(1)} %copy.9.touched, bf16[2,160,160]{2,1,0:T(8,128)(2,1)S(1)} %copy-done.3, bf16[2,160,160]{2,1,0:T(8,128)(2,1)S(1)} %copy-done.3, bf16[2,160,160]{2,1,0:T(8,128)(2,1)S(1)} %copy-done.5, ...), custom_call_target="tpu_custom_call" | custom-call | tf_op jit(solution)/shard_map/exchange/pallas_call | solution.py:447
  113.4 1.2 %copy.11 = f32[2,5,160,160]{3,2,1,0:T(8,128)} copy(f32[2,5,160,160]{3,2,1,0:T(8,128)S(1)} %exchange.1) | data formatting | bytes 2048000
Async XLA Ops:
  0.7 1.2 %copy-start = (bf16[2,4,256,256]{3,2,1,0:T(8,128)(2,1)S(1)}, bf16[2,4,256,256]{3,2,1,0:T(8,128)(2,1)}, u32[]{:S(2)}) copy-start(bf16[2,4,256,256]{3,2,1,0:T(8,128)(2,1)} %constant.14.clone.tzi) | copy-start | bytes 3145732
  2.0 1.2 %copy-start.1 = (bf16[2,4,256,256]{3,2,1,0:T(8,128)(2,1)S(1)}, bf16[2,4,256,256]{3,2,1,0:T(8,128)(2,1)}, u32[]{:S(2)}) copy-start(bf16[2,4,256,256]{3,2,1,0:T(8,128)(2,1)} %constant.13.clone.tz) | copy-start | bytes 3145732
  3.2 1.1 copy-start.2
  4.3 0.9 copy-start.3
  5.3 0.9 copy-start.4
  6.2 0.9 copy-start.5

commit v2 on v1

--- a/solution.py
+++ b/solution.py
@@ -17,8 +17,9 @@
 PL = 5
 ROWS = 32
 PACKED = 1008
-CHUNK = ((0, 256), (256, 256), (512, 256), (768, 240))
 FLOWS = ((0, 3, 0), (1, 2, 0), (1, 3, 1))
+COLUMNS = ((0, 0, 256), (1, 256, 256), (2, 512, 256), (3, 768, 240))
+MOST = 256
 FULL = 32000.0
 
 
@@ -31,13 +32,9 @@
     return jnp.dot(a, b, preferred_element_type=F32)
 
 
-def dot_left(table, x):
+def stack(x, axis):
     hi, lo = split(x)
-    return dot(table[0], hi) + dot(table[0], lo) + dot(table[1], hi)
-
-
-def dot_right(hi, lo, table):
-    return dot(hi, table[0]) + dot(lo, table[0]) + dot(hi, table[1])
+    return jnp.concatenate([hi, lo, hi], axis=axis)
 
 
 def exponent_of(largest):
@@ -65,9 +62,10 @@
 
 
 def kernel(
-    orb, touched, ty, tyi, tx, txi, tz, tzi, out,
+    orb_h, touched_h, ty_h, tx_h, txi_h, tz_h, tzi_h, out,
+    orb, touched, ty, tx, txi, tz, tzi, here,
     lend, seen, vis, relay_f, ret, ret_send, ret_got, relay_b,
-    c, send32, recv32, dhi, dlo, quant, grid_v,
+    c, send32, recv32, left, above, quant, grid_v,
     send_f, recv_f, send_b, recv_b,
     v_send, v_recv, vr_send, vr_recv, r_send, r_recv, rr_send, rr_recv,
     f_send, f_recv, b_send, b_recv,
@@ -78,17 +76,26 @@
     lane32 = iota((G, 128), 1)
     group32 = lane32 // 32
 
+    loads = [
+        pltpu.make_async_copy(src, dst, here.at[i])
+        for i, (src, dst) in enumerate(
+            zip((orb_h, ty_h, tx_h, txi_h, tz_h, tzi_h, touched_h), (orb, ty, tx, txi, tz, tzi, touched))
+        )
+    ]
+    for load in loads:
+        load.start()
+
     barrier = pltpu.get_barrier_semaphore()
 
     def greet_grid(i, _):
         pl.semaphore_signal(barrier, inc=1, device_id=(b, (g + i) % G), device_id_type=MESH)
         return 0
 
-    for d in range(1, 4):
-        pl.semaphore_signal(barrier, inc=1, device_id=(zh * 4 + (y + d) % 4, g), device_id_type=MESH)
     for block in (up, down):
         for yy in range(4):
             pl.semaphore_signal(barrier, inc=1, device_id=(block * 4 + yy, g), device_id_type=MESH)
+    for d in range(1, 4):
+        pl.semaphore_signal(barrier, inc=1, device_id=(zh * 4 + (y + d) % 4, g), device_id_type=MESH)
     lax.fori_loop(1, G, greet_grid, 0)
 
     def pack(plane, store):
@@ -113,8 +120,10 @@
             )
         return jnp.concatenate([main, tail], axis=1)
 
+    loads[0].wait()
+    loads[6].wait()
     for r in range(2):
-        chosen = touched[r, 0]
+        chosen = touched[0, r]
 
         def lent(x, chosen=chosen):
             pick = jnp.full((N, N), chosen, I32) == 0
@@ -124,6 +133,7 @@
             lend[r, start : start + size, :] = v.astype(BF16)
 
         put(6 * N, 48, pack(lent, put))
+
 
     pl.semaphore_wait(barrier, 42)
 
@@ -135,7 +145,12 @@
     def landed(ref, sem):
         pltpu.make_async_copy(ref, ref, sem).wait()
 
-    def ship(r, forward, src, dst, s, q, relay, rs, rq):
+    def crossing(r, forward):
+        for f, (fr, low, high) in enumerate(FLOWS):
+            if fr == r:
+                yield f, *((low, high) if forward else (high, low)), COLUMNS
+
+    def ship(r, forward, src, dst, s, q, relay, rq):
         ahead = r + 1 if forward else -r - 1
         inside = y + ahead < 4 if forward else y + ahead >= 0
         block = up if forward else down
@@ -144,14 +159,11 @@
         def _():
             copy(src.at[r], dst.at[r], s.at[r], q.at[r], (b + ahead, g)).start()
 
-        for f, (fr, low, high) in enumerate(FLOWS):
-            if fr != r:
-                continue
-            begin, end = (low, high) if forward else (high, low)
+        for f, begin, end, columns in crossing(r, forward):
 
             @pl.when(y == begin)
             def _():
-                for col, (start, size) in enumerate(CHUNK):
+                for col, start, size in columns:
                     part = src.at[r, pl.ds(start, size)]
                     if col == begin:
                         goal = dst.at[r, pl.ds(start, size)]
@@ -160,38 +172,32 @@
                         goal = relay.at[f, pl.ds(0, size)]
                         copy(part, goal, s.at[r], rq.at[f], (zh * 4 + col, g)).start()
 
+    def relays(r, forward, relay, act):
+        for f, begin, end, columns in crossing(r, forward):
+            for col, start, size in columns:
+                if col != begin:
+                    pl.when(y == col)(
+                        functools.partial(act, f, end, relay.at[f, pl.ds(0, size)], pl.ds(start, size))
+                    )
+
     def pass_on(r, forward, dst, q, relay, rs, rq):
         block = up if forward else down
-        for f, (fr, low, high) in enumerate(FLOWS):
-            if fr != r:
-                continue
-            begin, end = (low, high) if forward else (high, low)
-            for col, (start, size) in enumerate(CHUNK):
-                if col == begin:
-                    continue
-
-                @pl.when(y == col)
-                def _():
-                    part = relay.at[f, pl.ds(0, size)]
-                    landed(part, rq.at[f])
-                    goal = dst.at[r, pl.ds(start, size)]
-                    copy(part, goal, rs.at[f], q.at[r], (block * 4 + end, g)).start()
-
-    def shipped(forward, src, s, relay, rs):
+
+        def act(f, end, part, rows):
+            landed(part, rq.at[f])
+            copy(part, dst.at[r, rows], rs.at[f], q.at[r], (block * 4 + end, g)).start()
+
+        relays(r, forward, relay, act)
+
+    def passed(r, forward, relay, rs):
+        relays(r, forward, relay, lambda f, end, part, rows: landed(part, rs.at[f]))
+
+    def shipped(src, s):
         for r in range(2):
             landed(src.at[r], s.at[r])
-        for f, (fr, low, high) in enumerate(FLOWS):
-            begin = low if forward else high
-            for col, (start, size) in enumerate(CHUNK):
-                if col == begin:
-                    continue
-
-                @pl.when(y == col)
-                def _():
-                    landed(relay.at[f, pl.ds(0, size)], rs.at[f])
 
     for r in range(2):
-        ship(r, True, lend, seen, v_send, v_recv, relay_f, vr_send, vr_recv)
+        ship(r, True, lend, seen, v_send, v_recv, relay_f, vr_recv)
     for r in range(2):
         pass_on(r, True, seen, v_recv, relay_f, vr_send, vr_recv)
 
@@ -209,8 +215,6 @@
         factor = jnp.where(s > 0, (1.0 - jnp.exp(-safe)) / safe, 1.0)
         c[j] = factor * (100.0 / float(N) ** 3)
         return 0
-
-    lax.fori_loop(0, PL, fill, 0)
 
     def see(r):
         landed(seen.at[r], v_recv.at[r])
@@ -244,7 +248,7 @@
         def plane(x, carry):
             tail4, last = carry
             density = orb[band, x].astype(F32) * vis[r, x]
-            spread = dot_left((ty[0], ty[1]), density)
+            spread = dot(ty[...], stack(density, 0))
             largest = jnp.max(jnp.abs(spread), axis=1, keepdims=True)
             e = exponent_of(largest)
             q = jnp.round(spread * step_up(e))
@@ -261,7 +265,7 @@
             return tail4, last
 
         zero = jnp.zeros((G, 128), F32)
-        tail4, last = lax.fori_loop(0, PL, plane, (zero, zero))
+        tail4, last = lax.fori_loop(0, PL, plane, (zero, zero), unroll=True)
         send32[every(30, G), :] = tail4
         send32[every(31, G), :] = last
         send_f[a] = to_i16(send32[...])
@@ -290,30 +294,29 @@
             mixed = jnp.where(
                 group32 == 0, by[0], jnp.where(group32 == 1, by[1], jnp.where(group32 == 2, by[2], by[3]))
             )
-            t_hi, t_lo = split(recv32[every(25 + x, G), :] * mixed)
+            tail = split(recv32[every(25 + x, G), :] * mixed)
             for j in range(PL):
-                hi, lo = split(recv32[every(5 * x + j, G), :] * by[j])
-                dhi[j, rows, :128] = hi
-                dlo[j, rows, :128] = lo
+                main = split(recv32[every(5 * x + j, G), :] * by[j])
                 if j == 4:
-                    t_hi, t_lo = split(last_tail(x) * by[4])
-                dhi[j, rows, 128:] = t_hi
-                dlo[j, rows, 128:] = t_lo
-
-        def row(j, last):
-            v = j % 4
-            z = dot_right(dhi[j], dlo[j], (tz[0, v], tz[1, v]))
-            w = dot_left((tx[0], tx[1]), z) * c[j]
-            u = dot_left((txi[0], txi[1]), w)
-            hi, lo = split(u)
-            o = dot_right(hi, lo, (tzi[0, v], tzi[1, v]))
+                    tail = split(last_tail(x) * by[4])
+                for piece in range(3):
+                    at = 256 * piece
+                    left[j, rows, at : at + 128] = main[piece % 2]
+                    left[j, rows, at + 128 : at + 256] = tail[piece % 2]
+
+        for j in range(PL):
+            above[j] = stack(dot(left[j], tz[j % 4]), 0)
+        for j in range(PL):
+            above[j] = stack(dot(tx[...], above[j]) * c[j], 0)
+        for j in range(PL):
+            left[j] = stack(dot(txi[...], above[j]), 1)
+        last = jnp.zeros((G, 128), F32)
+        for j in range(PL):
+            o = dot(left[j], tzi[j % 4])
             e = exponent_of(jnp.max(jnp.abs(o), axis=1, keepdims=True))
             quant[j] = jnp.round(o * step_up(e))
             for x in range(PL):
                 last = jnp.where(lane32 == 32 + 5 * x + j, e[32 * x : 32 * x + 32], last)
-            return last
-
-        last = lax.fori_loop(0, PL, row, jnp.zeros((G, 128), F32))
         tail4 = jnp.zeros((G, 128), F32)
         for x in range(PL):
             rows = slice(32 * x, 32 * x + 32)
@@ -350,14 +353,14 @@
                 grid_v[x, rows, 128:] = tail * by
 
         def plane(x, _):
-            potential = dot_left((tyi[0], tyi[1]), grid_v[x])[:, :N]
+            potential = dot(ty[...], stack(grid_v[x], 0))[:, :N]
             added = vis[r, x] * potential
             back = orb[band, x].astype(F32) * potential
             out[band, x] = added if r == 0 else out[band, x] + added
             ret[x] = back if band == 0 else ret[x] + back
             return 0
 
-        lax.fori_loop(0, PL, plane, 0)
+        lax.fori_loop(0, PL, plane, 0, unroll=True)
 
     def give_back(r):
         exps = []
@@ -378,11 +381,11 @@
         for x in range(PL):
             last = jnp.where(free & (lane == 96 + x), exps[x], last)
         put(6 * N, 48, last)
-        ship(r, False, ret_send, ret_got, r_send, r_recv, relay_b, rr_send, rr_recv)
+        ship(r, False, ret_send, ret_got, r_send, r_recv, relay_b, rr_recv)
 
     def take_back(r):
         landed(ret_got.at[r], r_recv.at[r])
-        chosen = touched[r, 0]
+        chosen = touched[0, r]
         tail = step_down(ret_got[r, 6 * N : 6 * N + 48, :].astype(F32)[16:24])
         for x in range(PL):
             by = tail[0:1, 96 + x : 97 + x]
@@ -391,14 +394,22 @@
             out[0, x] = out[0, x] + jnp.where(mine, v, 0.0)
             out[1, x] = out[1, x] + jnp.where(mine, 0.0, v)
 
+    loads[1].wait()
     see(0)
     stage_a(0, 0)
     stage_a(0, 1)
+    for load in loads[2:6]:
+        load.wait()
+    lax.fori_loop(0, PL, fill, 0)
     see(1)
     stage_a(1, 0)
     stage_a(1, 1)
-    for a in range(4):
-        stage_b(a)
+
+    def slab(i, _):
+        stage_b(i)
+        return 0
+
+    lax.fori_loop(0, 4, slab, 0)
     stage_c(0, 0)
     stage_c(0, 1)
     give_back(0)
@@ -412,14 +423,17 @@
     for a in range(4):
         all_landed(a, send_f, f_send)
         all_landed(a, send_b, b_send)
-    shipped(True, lend, v_send, relay_f, vr_send)
-    shipped(False, ret_send, r_send, relay_b, rr_send)
-
-
-def pair(table):
+    shipped(lend, v_send)
+    shipped(ret_send, r_send)
+    for r in range(2):
+        passed(r, True, relay_f, vr_send)
+        passed(r, False, relay_b, rr_send)
+
+
+def pieces(table, axis):
     hi = table.astype(ml_dtypes.bfloat16)
     lo = (table - hi.astype(np.float64)).astype(ml_dtypes.bfloat16)
-    return np.stack([hi, lo])
+    return np.concatenate([hi, hi, lo], axis=axis)
 
 
 def tables():
@@ -427,7 +441,6 @@
     phase = (k[:, None] * k[None, :] % N) * (2.0 * np.pi / N)
     cas = np.cos(phase) + np.sin(phase)
     by_plane = (5 * np.arange(G)[None, :] + np.arange(PL)[:, None]).reshape(-1)
-    ty = cas
     tx = cas[:, by_plane]
     tz = np.zeros((4, 256, 256))
     tzi = np.zeros((4, 256, 256))
@@ -437,32 +450,42 @@
         tz[v, at : at + 32, :N] = cas[128:]
         tzi[v, :N, :128] = cas[:, :128]
         tzi[v, :N, at : at + 32] = cas[:, 128:]
-    return [pair(t) for t in (ty, ty.T, tx, tx.T, tz, tzi)]
+    left = [pieces(t, 1) for t in (cas, tx, tx.T)]
+    return left + [pieces(t, 1) for t in (tz, tzi)]
 
 
 def on_device(orbitals, touched):
-    vmem, smem = pl.BlockSpec(memory_space=pltpu.VMEM), pl.BlockSpec(memory_space=pltpu.SMEM)
+    vmem = pl.BlockSpec(memory_space=pltpu.VMEM)
+    hbm = pl.BlockSpec(memory_space=pltpu.HBM)
     dma = pltpu.SemaphoreType.DMA
     message = (4, G * ROWS, 128)
     return pl.pallas_call(
         kernel,
         out_shape=jax.ShapeDtypeStruct((2, PL, N, N), F32),
-        in_specs=[vmem, smem] + [vmem] * 6,
+        in_specs=[hbm] * 7,
         out_specs=vmem,
         scratch_shapes=[
+            pltpu.VMEM((2, PL, N, N), BF16),
+            pltpu.SMEM((1, 2), I32),
+            pltpu.VMEM((N, 3 * N), BF16),
+            pltpu.VMEM((N, 3 * N), BF16),
+            pltpu.VMEM((N, 3 * N), BF16),
+            pltpu.VMEM((4, 768, 256), BF16),
+            pltpu.VMEM((4, 768, 256), BF16),
+            dma((7,)),
             pltpu.VMEM((2, PACKED, 128), BF16),
             pltpu.VMEM((2, PACKED, 128), BF16),
             pltpu.VMEM((2, PL, N, N), F32),
-            pltpu.VMEM((3, 256, 128), BF16),
+            pltpu.VMEM((3, MOST, 128), BF16),
             pltpu.VMEM((PL, N, N), F32),
             pltpu.VMEM((2, PACKED, 128), I16),
             pltpu.VMEM((2, PACKED, 128), I16),
-            pltpu.VMEM((3, 256, 128), I16),
+            pltpu.VMEM((3, MOST, 128), I16),
             pltpu.VMEM((PL, N, 256), F32),
             pltpu.VMEM((G * ROWS, 128), F32),
             pltpu.VMEM((G * ROWS, 128), F32),
-            pltpu.VMEM((PL, N, 256), BF16),
-            pltpu.VMEM((PL, N, 256), BF16),
+            pltpu.VMEM((PL, N, 768), BF16),
+            pltpu.VMEM((PL, 3 * N, 256), BF16),
             pltpu.VMEM((PL, N, 256), F32),
             pltpu.VMEM((PL, N, 256), F32),
             pltpu.VMEM(message, I16),
@@ -474,10 +497,10 @@
             dma((4,)), dma((4,)), dma((4,)), dma((4,)),
         ],
         compiler_params=pltpu.CompilerParams(
-            collective_id=0, has_side_effects=True, vmem_limit_bytes=44 << 20
+            collective_id=0, has_side_effects=True, vmem_limit_bytes=60 << 20
         ),
         name="exchange",
-    )(orbitals, touched, *[jnp.asarray(t) for t in tables()])
+    )(orbitals, touched.T, *[jnp.asarray(t) for t in tables()])
 
 
 def solution(mesh):

time: 115 us -> 105 us (0.913)
  the two profiles are of different devices: /device:TPU:56 before, /device:TPU:81 now
where the time goes in v2:
time: 105 us
  Pallas kernels  103 us (98%)
  local copies, waits for them, and re-layouts  2.72 us (3%)
    pallas_call x1, Pallas kernels, on_device(): pl.pallas_call(kernel, out_shape=jax.ShapeDtypeStruct((2, PL, N, N), F32)...  103 us
    unnamed x1, local copies, waits for them, and re-layouts  2.72 us

profile of v2, /device:TPU:81, one launch (start us, length us, event | category | flops | bytes accessed | tf_op | source)
XLA Modules:
  0.0 105.3 jit_solution(10462375467316372326)
XLA Ops:
  0.0 102.5 %exchange.1 = f32[2,5,160,160]{3,2,1,0:T(8,128)} custom-call(bf16[2,5,160,160]{3,2,1,0:T(8,128)(2,1)} %orb_h.1, s32[1,2]{1,0:T(1,128)} %bitcast.1, bf16[160,480]{1,0:T(8,128)(2,1)} %constant.10.clone.ty_h, bf16[160,480]{1,0:T(8,128)(2,1)} %constant.11.clone.tx_h, bf16[160,480]{1,0:T(8,128)(2,1)} %constant.12.clone.txi_h, ...), custom_call_target="tpu_custom_call" | custom-call | tf_op jit(solution)/shard_map/exchange/pallas_call | solution.py:462
  102.6 2.7 %copy.9 = f32[2,5,160,160]{3,2,1,0:T(8,128)} copy(f32[2,5,160,160]{3,2,1,0:T(8,128)} %exchange.1) | data formatting | bytes 2048000

commit v3 on v2

--- a/solution.py
+++ b/solution.py
@@ -18,8 +18,12 @@
 ROWS = 32
 PACKED = 1008
 FLOWS = ((0, 3, 0), (1, 2, 0), (1, 3, 1))
-COLUMNS = ((0, 0, 256), (1, 256, 256), (2, 512, 256), (3, 768, 240))
-MOST = 256
+BITS, BIT = 2, 128
+COLUMNS = tuple(
+    (col, k, 256 * col + BIT * k, min(BIT, PACKED - 256 * col - BIT * k))
+    for k in range(BITS)
+    for col in range(4)
+)
 FULL = 32000.0
 
 
@@ -163,21 +167,21 @@
 
             @pl.when(y == begin)
             def _():
-                for col, start, size in columns:
+                for col, k, start, size in columns:
                     part = src.at[r, pl.ds(start, size)]
                     if col == begin:
                         goal = dst.at[r, pl.ds(start, size)]
                         copy(part, goal, s.at[r], q.at[r], (block * 4 + end, g)).start()
                     else:
-                        goal = relay.at[f, pl.ds(0, size)]
-                        copy(part, goal, s.at[r], rq.at[f], (zh * 4 + col, g)).start()
+                        goal = relay.at[f, pl.ds(BIT * k, size)]
+                        copy(part, goal, s.at[r], rq.at[BITS * f + k], (zh * 4 + col, g)).start()
 
     def relays(r, forward, relay, act):
         for f, begin, end, columns in crossing(r, forward):
-            for col, start, size in columns:
+            for col, k, start, size in columns:
                 if col != begin:
                     pl.when(y == col)(
-                        functools.partial(act, f, end, relay.at[f, pl.ds(0, size)], pl.ds(start, size))
+                        functools.partial(act, BITS * f + k, end, relay.at[f, pl.ds(BIT * k, size)], pl.ds(start, size))
                     )
 
     def pass_on(r, forward, dst, q, relay, rs, rq):
@@ -476,11 +480,11 @@
             pltpu.VMEM((2, PACKED, 128), BF16),
             pltpu.VMEM((2, PACKED, 128), BF16),
             pltpu.VMEM((2, PL, N, N), F32),
-            pltpu.VMEM((3, MOST, 128), BF16),
+            pltpu.VMEM((3, BITS * BIT, 128), BF16),
             pltpu.VMEM((PL, N, N), F32),
             pltpu.VMEM((2, PACKED, 128), I16),
             pltpu.VMEM((2, PACKED, 128), I16),
-            pltpu.VMEM((3, MOST, 128), I16),
+            pltpu.VMEM((3, BITS * BIT, 128), I16),
             pltpu.VMEM((PL, N, 256), F32),
             pltpu.VMEM((G * ROWS, 128), F32),
             pltpu.VMEM((G * ROWS, 128), F32),
@@ -492,8 +496,8 @@
             pltpu.VMEM(message, I16),
             pltpu.VMEM(message, I16),
             pltpu.VMEM(message, I16),
-            dma((2,)), dma((2,)), dma((3,)), dma((3,)),
-            dma((2,)), dma((2,)), dma((3,)), dma((3,)),
+            dma((2,)), dma((2,)), dma((3 * BITS,)), dma((3 * BITS,)),
+            dma((2,)), dma((2,)), dma((3 * BITS,)), dma((3 * BITS,)),
             dma((4,)), dma((4,)), dma((4,)), dma((4,)),
         ],
         compiler_params=pltpu.CompilerParams(

time: 105 us -> 105 us (level)
  the two profiles are of different devices: /device:TPU:81 before, /device:TPU:58 now
where the time goes in v3:
time: 105 us
  Pallas kernels  102 us (97%)
  local copies, waits for them, and re-layouts  2.72 us (3%)
    pallas_call x1, Pallas kernels, on_device(): pl.pallas_call(kernel, out_shape=jax.ShapeDtypeStruct((2, PL, N, N), F32)...  102 us
    unnamed x1, local copies, waits for them, and re-layouts  2.72 us

profile of v3, /device:TPU:58, one launch (start us, length us, event | category | flops | bytes accessed | tf_op | source)
XLA Modules:
  0.0 105.2 jit_solution(760390833742580646)
XLA Ops:
  0.0 102.4 %exchange.1 = f32[2,5,160,160]{3,2,1,0:T(8,128)} custom-call(bf16[2,5,160,160]{3,2,1,0:T(8,128)(2,1)} %orb_h.1, s32[1,2]{1,0:T(1,128)} %bitcast.1, bf16[160,480]{1,0:T(8,128)(2,1)} %constant.10.clone.ty_h, bf16[160,480]{1,0:T(8,128)(2,1)} %constant.11.clone.tx_h, bf16[160,480]{1,0:T(8,128)(2,1)} %constant.12.clone.txi_h, ...), custom_call_target="tpu_custom_call" | custom-call | tf_op jit(solution)/shard_map/exchange/pallas_call | solution.py:466
  102.4 2.7 %copy.9 = f32[2,5,160,160]{3,2,1,0:T(8,128)} copy(f32[2,5,160,160]{3,2,1,0:T(8,128)} %exchange.1) | data formatting | bytes 2048000
